TPU v7x, 128 devices: a whole 4x4x4 slice. The times are simulated.
128 devices in a mesh: blk: 64 (over x, z_lo, y, core), split: 2 (over z_hi).
Axes of the slice: x: 4, y: 4, z: 4 (z_hi: 2, z_lo: 2; z = z_hi * 2 + z_lo), core: 2. Of those that a mesh axis runs over, the one named last changes fastest.
Arguments:
- queries: bfloat16 [64, 512, 1024], P('blk'), may hold values from -54 to 54
- prefix_kv: bfloat16 [16384, 256], P(('blk', 'split')), may hold values from -12 to 12
- suffix_kv: bfloat16 [64, 512, 256], P('blk', 'split'), may hold values from -6 to 6
Outputs:
- attended: bfloat16 [64, 512, 1024], P('blk', None, 'split')
All inputs are finite; a program needn't handle non-finite values.
Results may differ from a plain program's by a relative error of at most 0.018.
Values may be sent and summed in bfloat16 or wider, within the bound.
A program may use at most 64 MiB of HBM per device.

v0:
```python
import math

import jax
import jax.numpy as jnp
from jax import lax
from jax.sharding import PartitionSpec as P


def suffix_part(query_block, own_kv, offset, heads_here, scale):
    head_size = query_block.shape[2]
    key_part = own_kv[:, :, :head_size]
    value_part = own_kv[:, :, head_size:]
    scores = (
        jnp.einsum("brd,bnd->brn", query_block, key_part, preferred_element_type=jnp.float32)
        * scale
    )
    token_pos = lax.iota(jnp.int32, query_block.shape[1]) // heads_here
    key_pos = offset + lax.iota(jnp.int32, own_kv.shape[1])
    allowed = (key_pos[None, :] <= token_pos[:, None])[None]
    scores = jnp.where(allowed, scores, -1e30)
    running_max = scores.max(axis=2)
    weights = jnp.where(allowed, jnp.exp(scores - running_max[:, :, None]), 0.0)
    running_sum = weights.sum(axis=2)
    weighted = jnp.einsum(
        "brn,bnd->brd", weights.astype(jnp.bfloat16), value_part, preferred_element_type=jnp.float32
    )
    return (running_max.reshape(-1), running_sum.reshape(-1), weighted.reshape(-1, head_size))


def absorb(carried, piece, query_rows, scale):
    head_size = query_rows.shape[1]
    count = piece.shape[0]
    block_len = 512
    tiles = piece.reshape(count // block_len, block_len, piece.shape[1])

    def scan_step(state, tile_kv):
        running_max, running_sum, weighted = state
        scores = (
            jnp.einsum(
                "rd,nd->rn", query_rows, tile_kv[:, :head_size], preferred_element_type=jnp.float32
            )
            * scale
        )
        new_max = jnp.maximum(running_max, scores.max(axis=1))
        correction = jnp.exp(running_max - new_max)
        weights = jnp.exp(scores - new_max[:, None])
        running_sum = running_sum * correction + weights.sum(axis=1)
        weighted = weighted * correction[:, None] + jnp.dot(
            weights.astype(jnp.bfloat16), tile_kv[:, head_size:], preferred_element_type=jnp.float32
        )
        return ((new_max, running_sum, weighted), None)

    final_state, unused = lax.scan(scan_step, carried, tiles)
    return final_state


def prefix_pass(query_rows, block, carried, scale):
    return absorb(carried, lax.all_gather(block, "blk", axis=0, tiled=True), query_rows, scale)


def shards(queries, prefix_kv, suffix_kv):
    head_size = prefix_kv.shape[1] // 2
    suf_count, suffix_len, width = queries.shape
    heads = width // head_size
    scale = 1.0 / math.sqrt(head_size)
    query_block = queries.reshape(suf_count, suffix_len * heads, head_size)
    offset = lax.axis_index("split") * suffix_kv.shape[1]
    carried = suffix_part(query_block, suffix_kv, offset, heads, scale)
    running_max, running_sum, weighted = prefix_pass(
        query_block.reshape(-1, head_size), prefix_kv, carried, scale
    )
    global_max = lax.pmax(running_max, "split")
    factor = jnp.exp(running_max - global_max)
    numerator = (weighted * factor[:, None]).reshape(suf_count * suffix_len, heads * head_size)
    denominator = (running_sum * factor).reshape(suf_count * suffix_len, heads)
    numerator, denominator = (
        lax.psum_scatter(
            numerator.astype(jnp.bfloat16), "split", scatter_dimension=1, tiled=True
        ).astype(jnp.float32),
        lax.psum_scatter(
            denominator.astype(jnp.bfloat16), "split", scatter_dimension=1, tiled=True
        ).astype(jnp.float32),
    )
    heads_here = denominator.shape[1]
    result = (
        numerator.reshape(suf_count * suffix_len, heads_here, head_size) / denominator[:, :, None]
    )
    return result.reshape(suf_count, suffix_len, heads_here * head_size).astype(jnp.bfloat16)


def solution(mesh):
    in_specs = (P("blk", None, None), P(("blk", "split"), None), P("blk", "split", None))
    out_specs = P("blk", None, "split")
    return jax.shard_map(shards, mesh=mesh, in_specs=in_specs, out_specs=out_specs, check_vma=False)
```

profile of v0, /device:TPU:1, one launch (start us, length us, event | category | flops | bytes accessed | tf_op | source)
XLA Modules:
  0.0 261.1 jit_solution(16301085108234261257)
XLA Ops:
  7.3 1.5 reshape.66
  8.9 1.6 fusion.28
  12.5 106.1 %all-gather.2.cloned.1.call-done = bf16[8192,256]{1,0:T(8,128)(2,1)} async-done(((bf16[128,256]{1,0:T(8,128)(2,1)}), bf16[8192,256]{1,0:T(8,128)(2,1)}) %all-gather.2.cloned.1.call-update) | async-done | bytes 4194320 | tf_op jit(solution)/shard_map/all_gather | solution.py:58
  118.6 98.0 %while.14 = (s32[]{:T(128)}, f32[4096]{0:T(1024)S(1)}, f32[4096]{0:T(1024)S(1)}, f32[4096,128]{1,0:T(8,128)S(1)}, bf16[16,512,256]{2,1,0:T(8,128)(2,1)}, /*index=5*/bf16[4096,128]{1,0:T(8,128)(2,1)S(1)}, s32[]{:T(128)}) while((s32[]{:T(128)}, f32[4096]{0:T(1024)S(1)}, f32[4096]{0:T(1024)S(1)}, f32[4096,128]{1,0:T(8,128)S(1)}, ...), condition=%wide.region_5.6_spmd, body=%wide.region_2.5_spmd.sunk | while | flops 1091575808 | bytes 31457360 | solution.py:53
  122.3 2.4 convolution_add_fusion.2
  128.4 2.4 convolution_add_fusion.2
  134.5 2.4 convolution_add_fusion.2
  140.7 2.4 convolution_add_fusion.2
  146.8 2.4 convolution_add_fusion.2
  152.9 2.4 convolution_add_fusion.2
  159.0 2.4 convolution_add_fusion.2
  165.2 2.4 convolution_add_fusion.2
  171.3 2.4 convolution_add_fusion.2
  177.4 2.4 convolution_add_fusion.2
  183.6 2.4 convolution_add_fusion.2
  189.7 2.4 convolution_add_fusion.2
  195.8 2.4 convolution_add_fusion.2
  201.9 2.4 convolution_add_fusion.2
  208.1 2.4 convolution_add_fusion.2
  214.2 2.4 convolution_add_fusion.2
  216.6 8.9 %pmax.7 = f32[4096]{0:T(1024)S(1)} all-reduce(f32[4096]{0:T(1024)S(1)} %get-tuple-element.40), channel_id=1, replica_groups=mesh['blk'=64,'split'=2] {'split'}, use_global_device_ids=true, to_apply=%region_6.7 | all-reduce | flops 4096 | bytes 32768 | tf_op jit(solution)/shard_map/pmax | solution.py:72
  229.0 8.9 %all-reduce = bf16[512,8]{1,0:T(8,128)(2,1)S(1)} all-reduce(bf16[512,8]{1,0:T(8,128)(2,1)S(1)} %convert_element_type.37), channel_id=3, replica_groups=mesh['blk'=64,'split'=2] {'split'}, use_global_device_ids=true, to_apply=%region_8.9.clone | all-reduce | flops 4096 | bytes 16384
  238.0 13.6 %reduce-scatter.3.cloned.1.call-done = bf16[512,512]{1,0:T(8,128)(2,1)} async-done(((bf16[512,1024]{1,0:T(8,128)(2,1)}), bf16[512,512]{1,0:T(8,128)(2,1)}) %reduce-scatter.3.cloned.1.call-update) | async-done | bytes 524304 | tf_op jit(solution)/shard_map/reduce_scatter | solution.py:77
  252.2 2.1 fusion.19
  (115 shorter events, 64.6 us)
Async XLA Ops:
  6.5 112.1 %all-gather.2.cloned.1.call-start = ((), (), s32[]{:S(2)}) async-start(), calls=%async_computation.1 | async-start | bytes 4259840 | tf_op jit(solution)/shard_map/all_gather | solution.py:58
  7.3 244.3 %reduce-scatter.3.cloned.1.call-start = ((), (), s32[]{:S(2)}) async-start(), calls=%async_computation.2 | async-start | bytes 1572864 | tf_op jit(solution)/shard_map/reduce_scatter | solution.py:77
  10.5 0.9 copy-start
  216.6 10.9 %copy-start.1 = (u32[128]{0:T(128)S(1)}, u32[128]{0:T(128)}, u32[]{:S(2)}) copy-start(u32[128]{0:T(128)} %constant.50) | copy-start | bytes 1540
Sparse Core Ops, SparseCore 0:
  9.1 109.4 all-gather.1
  227.7 23.8 reduce-scatter.2
where the time goes:
time: 262 us; the launch traced here: 261 us
  waiting for transfers between devices  120 us (46%)
  matrix products  61.7 us (24%)
  other arithmetic  26.2 us (10%)
  local copies, waits for them, and re-layouts  19.8 us (8%)
  blocking collectives  17.8 us (7%)
  between operations  14.2 us (5%)
    all_gather x1, waiting for transfers between devices, prefix_pass(): lax.all_gather(block, 'blk', axis=0, tiled=True)  106 us
    dot_general x16, matrix products, scan_step(): jnp.dot(weights.astype(jnp.bfloat16), tile_kv[:, head_size:], preferred_e...  38.7 us
    reduce_sum x16, other arithmetic, scan_step(): running_sum = running_sum * correction + weights.sum(axis=1)  22.2 us
    dot_general x16, matrix products, scan_step(): jnp.einsum('rd,nd->rn', query_rows, tile_kv[:, :head_size], preferred_ele...  20.3 us
    squeeze x16, local copies, waits for them, and re-layouts, absorb(): final_state, unused = lax.scan(scan_step, carried, tiles)  15.5 us
    reduce_scatter x1, waiting for transfers between devices, shards(): lax.psum_scatter(numerator.astype(jnp.bfloat16), 'split', scatter_dimensi...  13.6 us
    unnamed x1, blocking collectives  8.89 us
    pmax x1, blocking collectives, shards(): global_max = lax.pmax(running_max, 'split')  8.87 us
  transfers between devices with their start and end apart: 2, of which 2 were waited for; matrix products, arithmetic and copies ran while one was open for 2% of the time, Pallas kernels for 0%

commit v1 on v0

v1 whole, which is shorter than its diff:
```python
import functools
import math

import jax
import jax.numpy as jnp
from jax import lax
from jax.experimental import pallas as pl
from jax.experimental.pallas import tpu as pltpu
from jax.sharding import PartitionSpec as P

MESH = pl.DeviceIdType.MESH
D = 128
SUB = 8
LANES = 256
LINE = 4
BLOCK = 128
TOKENS = 2 * LINE * BLOCK
PIECES = 4
PIECE = TOKENS // PIECES
LOG2E = 1.4426950408889634
NEG = -1e30


def gray(i):
    return i + (i // 2) * (1 - 2 * (i % 2))


def kernel(
    q_hbm, prefix_ref, suffix_ref, out_ref,
    kv, q_in, q_t, other, s0, s1, p0, p1, x0, x1, c0, c1, m_ref, l_ref, acc,
    q_sem, send_sem, recv_sem, line_sem, sib_sem,
):
    scale = LOG2E / math.sqrt(D)
    scores, weights, tops, fixes = (s0, s1), (p0, p1), (x0, x1), (c0, c1)
    tokens_here = suffix_ref.shape[1]
    seq, width = q_in.shape
    heads = width // D
    rows = heads * seq
    units = rows // LANES

    blk, split = lax.axis_index("blk"), lax.axis_index("split")
    core = blk % 2
    x, y, z = blk // 16, (blk // 2) % 4, split * 2 + (blk // 8) % 2

    def device(d1=0, d2=0, d3=0, other_core=0):
        nx = (x + d1 * (1 - core) + d3 * core) % 4
        ny = (y + d2) % 4
        nz = (z + d1 * core + d3 * (1 - core)) % 4
        nc = (core + other_core) % 2
        return (nx * 16 + (nz % 2) * 8 + ny * 2 + nc, nz // 2)

    a1 = x * (1 - core) + z * core
    a3 = z * (1 - core) + x * core
    sibling = device(other_core=1)
    partner = ((x * 16 + (z % 2) * 8 + y * 2 + core), 1 - split)
    peers = [device(d1=1), device(d1=2), device(d1=3), device(d2=1), device(d2=3), device(d3=1), device(d3=3)]

    barrier = pltpu.get_barrier_semaphore()
    for peer in peers + [sibling, partner]:
        pl.semaphore_signal(barrier, inc=1, device_id=peer, device_id_type=MESH)

    q_copy = pltpu.make_async_copy(
        q_hbm.at[0, :, pl.ds(pl.multiple_of(split * width, width), width)], q_in, q_sem
    )
    q_copy.start()

    kv[core, a3, y, a1, 0] = prefix_ref[:, :D]
    kv[core, a3, y, a1, 1] = prefix_ref[:, D:].astype(jnp.float32).T.astype(jnp.bfloat16)

    m_ref[...] = jnp.full_like(m_ref, NEG)
    l_ref[...] = jnp.zeros_like(l_ref)
    acc[...] = jnp.zeros_like(acc)
    p1[...] = jnp.zeros_like(p1)
    c1[...] = jnp.ones_like(c1)

    pl.semaphore_wait(barrier, 9)

    def remote(src, dst, send, recv, target):
        return pltpu.make_async_remote_copy(
            src_ref=src, dst_ref=dst, send_sem=send, recv_sem=recv, device_id=target, device_id_type=MESH
        )

    def first(d):
        here = kv.at[core, a3, y, a1]
        return remote(here, here, send_sem.at[d - 1], recv_sem.at[3 - d], device(d1=d))

    def line_at(d3, d2):
        return kv.at[core, (a3 + d3) % 4, (y + d2) % 4]

    sends = []

    def line_copy(index, d3, d2, s3, s2):
        ref = line_at(d3, d2)
        landing = ((d3 - s3) % 4) * 4 + (d2 - s2) % 4
        return remote(ref, ref, send_sem.at[3 + index], line_sem.at[landing], device(d3=s3 % 4, d2=s2 % 4))

    def sib_copy(d3, d2):
        ref = line_at(d3, d2)
        return remote(ref, ref, send_sem.at[19 + d3 * 4 + d2], sib_sem.at[d3 * 4 + d2], sibling)

    def other_copy():
        return remote(suffix_ref.at[0], other, send_sem.at[18], recv_sem.at[3], partner)

    plan = [
        (0, 0, 0, 1), (0, 0, 0, -1), (0, 3, 0, 1),
        (0, 0, 1, 0), (0, 0, -1, 0), (0, 1, 1, 0), (0, 1, -1, 0),
        (0, 3, 1, 0), (0, 3, -1, 0), (0, 2, 1, 0), (0, 2, -1, 0),
        (3, 0, 1, 0), (3, 1, 1, 0), (1, 2, -1, 0), (1, 3, -1, 0),
    ]

    def event(d3, d2):
        if (d3, d2) == (0, 0):
            for d in (1, 2, 3):
                first(d).wait_recv()
        else:
            ref = line_at(d3, d2)
            remote(ref, ref, send_sem.at[3], line_sem.at[d3 * 4 + d2], sibling).wait_recv()
        for index, (e3, e2, s3, s2) in enumerate(plan):
            if (e3, e2) == (d3, d2):
                line_copy(index, e3, e2, s3, s2).start()
        sib_copy(d3, d2).start()

    def sib_wait(d3, d2):
        ref = kv.at[1 - core, (a1 + d3) % 4, (y + d2) % 4]
        remote(ref, ref, send_sem.at[3], sib_sem.at[d3 * 4 + d2], sibling).wait_recv()

    for d in (1, 2, 3):
        first(d).start()
    other_copy().start()

    q_copy.wait()
    for h in range(heads):
        q_t[:, h * seq : (h + 1) * seq] = q_in[:, h * D : (h + 1) * D].astype(jnp.float32).T.astype(jnp.bfloat16)

    def cols(b):
        return slice(b * LANES, (b + 1) * LANES)

    def tile_max(s):
        return jnp.max(s.reshape(s.shape[0] // SUB, SUB, LANES), axis=0)

    def own_part(keys, values_t, offset):
        for b in range(units):
            s = jnp.dot(keys, q_t[:, cols(b)], preferred_element_type=jnp.float32)
            u = lax.broadcasted_iota(jnp.int32, s.shape, 0) + offset
            t = lax.broadcasted_iota(jnp.int32, s.shape, 1) + (b * LANES) % seq
            s = jnp.where(u <= t, s, NEG)
            m_old = m_ref[:, cols(b)]
            m_new = jnp.maximum(m_old, jnp.max(tile_max(s), axis=0, keepdims=True) * scale)
            fix = jnp.exp2(m_old - m_new)
            m_ref[:, cols(b)] = m_new
            p = jnp.exp2(s * scale - m_new)
            l_ref[:, cols(b)] = l_ref[:, cols(b)] * fix + jnp.sum(p.reshape(-1, SUB, LANES), axis=0)
            acc[:, cols(b)] = acc[:, cols(b)] * fix + jnp.dot(
                values_t, p.astype(jnp.bfloat16), preferred_element_type=jnp.float32
            )

    def values_of(ref):
        return ref[:, D:].astype(jnp.float32).T.astype(jnp.bfloat16)

    own_part(suffix_ref[0, :, :D], values_of(suffix_ref.at[0]), split * tokens_here)

    def lines(i):
        d3, d2 = gray(i // 4), gray(i % 4)
        return (core, (a3 + d3) % 4, (y + d2) % 4), (1 - core, (a1 + d3) % 4, (y + d2) % 4)

    def keys_of(i, j):
        c, l3, l2 = lines(i)[j // 2]
        k = 2 * (j % 2)
        return kv[c, l3, l2, pl.ds(k, 2), 0].reshape(PIECE, D)

    def qk(i, b, buf, j, top):
        s = jnp.dot(keys_of(i, j), q_t[:, cols(b)], preferred_element_type=jnp.float32)
        scores[buf][j * PIECE : (j + 1) * PIECE, :] = s
        here = tile_max(s)
        return here if top is None else jnp.maximum(top, here)

    def pv(i, buf):
        parts = []
        for c, l3, l2 in lines(i):
            parts += [kv[c, l3, l2, k, 1] for k in range(LINE)]
        return jnp.dot(jnp.concatenate(parts, axis=1), weights[buf][...], preferred_element_type=jnp.float32)

    last = 15

    def unit(i, b):
        ni, nb = (i, b + 1) if b < units - 1 else (jnp.minimum(i + 1, last), 0)
        pi, pb = (i, b - 1) if b > 0 else (jnp.maximum(i - 1, 0), units - 1)
        buf, nbuf = b % 2, (b + 1) % 2
        m_old = m_ref[:, cols(b)]
        m_new = jnp.maximum(m_old, jnp.max(tops[buf][...], axis=0, keepdims=True) * scale)
        fix = jnp.exp2(m_old - m_new)
        m_ref[:, cols(b)] = m_new
        fixes[buf][...] = fix
        total = l_ref[:, cols(b)] * fix
        top, add = None, None
        for j in range(PIECES):
            top = qk(ni, nb, nbuf, j, top)
            if j == 0:
                add = pv(pi, nbuf)
            part = slice(j * PIECE, (j + 1) * PIECE)
            p = jnp.exp2(scores[buf][part, :] * scale - m_new)
            weights[buf][part, :] = p.astype(jnp.bfloat16)
            total = total + jnp.sum(p.reshape(-1, SUB, LANES), axis=0)
        tops[nbuf][...] = top
        l_ref[:, cols(b)] = total
        acc[:, cols(pb)] = acc[:, cols(pb)] * fixes[nbuf][...] + add

    handed = {
        0: [(0, 3), (0, 1), (3, 0), (1, 0)],
        1: [(3, 1), (1, 3), (3, 3), (1, 1)],
        2: [(0, 2), (2, 0)],
        3: [(3, 2), (1, 2)],
        4: [(2, 1), (2, 3)],
        5: [(2, 2)],
    }

    event(0, 0)
    sib_wait(0, 0)
    top = None
    for j in range(PIECES):
        top = qk(0, 0, 0, j, top)
    tops[0][...] = top

    def body(i, carry):
        for b in range(units):
            if b == units // 2:
                for step, group in handed.items():
                    @pl.when(i == step)
                    def _(group=group):
                        for d3, d2 in group:
                            event(d3, d2)
            if b == units - 1:
                for step in range(1, 16):
                    @pl.when(i + 1 == step)
                    def _(step=step):
                        sib_wait(gray(step // 4), gray(step % 4))
            unit(i, b)
        return carry

    lax.fori_loop(0, 16, body, 0)
    pb = units - 1
    acc[:, cols(pb)] = acc[:, cols(pb)] * fixes[pb % 2][...] + pv(last, pb % 2)

    other_copy().wait_recv()
    own_part(other[:, :D], values_of(other), (1 - split) * tokens_here)

    for h in range(heads):
        part = slice(h * seq, (h + 1) * seq)
        inverse = 1.0 / jnp.sum(l_ref[:, part], axis=0, keepdims=True)
        out_ref[0, :, h * D : (h + 1) * D] = (acc[:, part] * inverse).T.astype(jnp.bfloat16)

    for d in (1, 2, 3):
        first(d).wait_send()
    other_copy().wait_send()
    for index, (e3, e2, s3, s2) in enumerate(plan):
        line_copy(index, e3, e2, s3, s2).wait_send()
    for d3 in range(4):
        for d2 in range(4):
            sib_copy(d3, d2).wait_send()


def shards(queries, prefix_kv, suffix_kv):
    suf_count, seq, width = queries.shape
    half = width // 2
    rows = (half // D) * seq
    vmem = pl.BlockSpec(memory_space=pltpu.VMEM)
    return pl.pallas_call(
        kernel,
        out_shape=jax.ShapeDtypeStruct((suf_count, seq, half), jnp.bfloat16),
        in_specs=[pl.BlockSpec(memory_space=pl.ANY), vmem, vmem],
        out_specs=vmem,
        scratch_shapes=[
            pltpu.VMEM((2, 4, 4, LINE, 2, BLOCK, D), jnp.bfloat16),
            pltpu.VMEM((seq, half), jnp.bfloat16),
            pltpu.VMEM((D, rows), jnp.bfloat16),
            pltpu.VMEM(suffix_kv.shape[1:], jnp.bfloat16),
            pltpu.VMEM((TOKENS, LANES), jnp.float32),
            pltpu.VMEM((TOKENS, LANES), jnp.float32),
            pltpu.VMEM((TOKENS, LANES), jnp.bfloat16),
            pltpu.VMEM((TOKENS, LANES), jnp.bfloat16),
            pltpu.VMEM((SUB, LANES), jnp.float32),
            pltpu.VMEM((SUB, LANES), jnp.float32),
            pltpu.VMEM((1, LANES), jnp.float32),
            pltpu.VMEM((1, LANES), jnp.float32),
            pltpu.VMEM((1, rows), jnp.float32),
            pltpu.VMEM((SUB, rows), jnp.float32),
            pltpu.VMEM((D, rows), jnp.float32),
            pltpu.SemaphoreType.DMA,
            pltpu.SemaphoreType.DMA((35,)),
            pltpu.SemaphoreType.DMA((4,)),
            pltpu.SemaphoreType.DMA((16,)),
            pltpu.SemaphoreType.DMA((16,)),
        ],
        compiler_params=pltpu.CompilerParams(
            collective_id=0, has_side_effects=True, vmem_limit_bytes=48 * 2**20
        ),
        cost_estimate=pl.CostEstimate(flops=17 * 10**9, bytes_accessed=2 * 2**20, transcendentals=34 * 10**6),
    )(queries, prefix_kv, suffix_kv)


def solution(mesh):
    in_specs = (P("blk", None, None), P(("blk", "split"), None), P("blk", "split", None))
    out_specs = P("blk", None, "split")
    return jax.shard_map(shards, mesh=mesh, in_specs=in_specs, out_specs=out_specs, check_vma=False)
```

time: 262 us -> 84.9 us (0.32)
  waiting for transfers between devices: 120 us -> 0 us
  Pallas kernels: 0 us -> 80.9 us
  matrix products: 61.7 us -> 0 us
  other arithmetic: 26.2 us -> 0 us
  blocking collectives: 17.8 us -> 0 us
  local copies, waits for them, and re-layouts: 19.8 us -> 3.76 us
  between operations: 14.2 us -> 0.01 us
    all_gather x1 -> x0, waiting for transfers between devices: 106 us -> none  [prefix_pass(): lax.all_gather(block, 'blk', axis=0, tiled=True)]
    pallas_call x0 -> x1, Pallas kernels: none -> 80.9 us  [shards(): pl.pallas_call(kernel, out_shape=jax.ShapeDtypeStruct((suf_count, seq, ha...]
    dot_general x34 -> x0, matrix products: 61.7 us -> none  [the longest x16 38.7 us: scan_step(): jnp.dot(weights.astype(jnp.bfloat16), tile_kv[:, head_size:], preferred_e...]
    reduce_sum x17 -> x0, other arithmetic: 23 us -> none  [the longest x16 22.2 us: scan_step(): running_sum = running_sum * correction + weights.sum(axis=1)]
    squeeze x16 -> x0, local copies, waits for them, and re-layouts: 15.5 us -> none  [absorb(): final_state, unused = lax.scan(scan_step, carried, tiles)]
    reduce_scatter x1 -> x0, waiting for transfers between devices: 13.6 us -> none  [shards(): lax.psum_scatter(numerator.astype(jnp.bfloat16), 'split', scatter_dimensi...]
    unnamed x1 -> x0, blocking collectives: 8.89 us -> none
    pmax x1 -> x0, blocking collectives: 8.87 us -> none  [shards(): global_max = lax.pmax(running_max, 'split')]
  transfers between devices with their start and end apart: 2 -> 0, of which waited for: 2 -> 0; matrix products, arithmetic and copies ran while one was open for 2% -> 0% of each run, Pallas kernels for 0% -> 0%
where the time goes in v1:
time: 84.9 us; the launch traced here: 84.7 us
  Pallas kernels  80.9 us (95%)
  local copies, waits for them, and re-layouts  3.76 us (4%)
    pallas_call x1, Pallas kernels, shards(): pl.pallas_call(kernel, out_shape=jax.ShapeDtypeStruct((suf_count, seq, ha...  80.9 us
    unnamed x7, local copies, waits for them, and re-layouts  3.76 us

profile of v1, /device:TPU:1, one launch (start us, length us, event | category | flops | bytes accessed | tf_op | source)
XLA Modules:
  0.0 84.7 jit_solution(8739315082190224141)
XLA Ops:
  0.0 0.0 copy-start
  0.0 1.2 %copy-done = bf16[1,512,1024]{2,1,0:T(8,128)(2,1)S(1)} copy-done((bf16[1,512,1024]{2,1,0:T(8,128)(2,1)S(1)}, bf16[1,512,1024]{2,1,0:T(8,128)(2,1)}, u32[]{:S(2)}) %copy-start) | copy-done | bytes 1048600
  1.2 0.0 copy-start.1
  1.2 0.9 %copy-done.1 = bf16[1,256,256]{2,1,0:T(8,128)(2,1)S(1)} copy-done((bf16[1,256,256]{2,1,0:T(8,128)(2,1)S(1)}, bf16[1,256,256]{2,1,0:T(8,128)(2,1)}, u32[]{:S(2)}) %copy-start.1) | copy-done | bytes 131096
  2.1 0.0 copy-start.2
  2.1 0.8 copy-done.2
  3.0 80.9 %shard_map.37 = bf16[1,512,512]{2,1,0:T(8,128)(2,1)S(1)} custom-call(bf16[1,512,1024]{2,1,0:T(8,128)(2,1)S(1)} %copy-done, bf16[128,256]{1,0:T(8,128)(2,1)S(1)} %copy-done.2, bf16[1,256,256]{2,1,0:T(8,128)(2,1)S(1)} %copy-done.1), custom_call_target="tpu_custom_call" | custom-call | flops 16999999488 | bytes 2097152 | tf_op jit(solution)/shard_map/pallas_call | solution.py:267
  83.9 0.8 copy.5
Async XLA Ops:
  0.0 1.2 %copy-start = (bf16[1,512,1024]{2,1,0:T(8,128)(2,1)S(1)}, bf16[1,512,1024]{2,1,0:T(8,128)(2,1)}, u32[]{:S(2)}) copy-start(bf16[1,512,1024]{2,1,0:T(8,128)(2,1)} %q_hbm.1) | copy-start | bytes 3145732
  1.2 0.9 %copy-start.1 = (bf16[1,256,256]{2,1,0:T(8,128)(2,1)S(1)}, bf16[1,256,256]{2,1,0:T(8,128)(2,1)}, u32[]{:S(2)}) copy-start(bf16[1,256,256]{2,1,0:T(8,128)(2,1)} %suffix_ref.1) | copy-start | bytes 393220
  2.1 0.8 copy-start.2

commit v2 on v1

--- a/solution.py
+++ b/solution.py
@@ -21,18 +21,14 @@
 NEG = -1e30
 
 
-def gray(i):
-    return i + (i // 2) * (1 - 2 * (i % 2))
-
-
 def kernel(
-    q_hbm, prefix_ref, suffix_ref, out_ref,
-    kv, q_in, q_t, other, s0, s1, p0, p1, x0, x1, c0, c1, m_ref, l_ref, acc,
-    q_sem, send_sem, recv_sem, line_sem, sib_sem,
+    q_hbm, prefix_hbm, suffix_hbm, out_ref,
+    kv, q_in, q_t, prefix_ref, suffix_ref, other, s0, s1, p0, p1, x0, x1, c0, c1, m_ref, l_ref, acc,
+    in_sem, send_sem, first_sem, line_sem, sib_sem,
 ):
     scale = LOG2E / math.sqrt(D)
     scores, weights, tops, fixes = (s0, s1), (p0, p1), (x0, x1), (c0, c1)
-    tokens_here = suffix_ref.shape[1]
+    tokens_here = suffix_ref.shape[0]
     seq, width = q_in.shape
     heads = width // D
     rows = heads * seq
@@ -53,81 +49,91 @@
     a3 = z * (1 - core) + x * core
     sibling = device(other_core=1)
     partner = ((x * 16 + (z % 2) * 8 + y * 2 + core), 1 - split)
-    peers = [device(d1=1), device(d1=2), device(d1=3), device(d2=1), device(d2=3), device(d3=1), device(d3=3)]
-
+    copies_here = [device(**{axis: d}) for axis in ("d1", "d2", "d3") for d in (1, 2, 3)]
+    copies_here += [device(d3=d, other_core=1) for d in (1, 2, 3)] + [sibling, partner]
     barrier = pltpu.get_barrier_semaphore()
-    for peer in peers + [sibling, partner]:
+    for peer in copies_here:
         pl.semaphore_signal(barrier, inc=1, device_id=peer, device_id_type=MESH)
 
+    prefix_copy = pltpu.make_async_copy(prefix_hbm, prefix_ref, in_sem.at[0])
+    suffix_copy = pltpu.make_async_copy(suffix_hbm.at[0], suffix_ref, in_sem.at[1])
     q_copy = pltpu.make_async_copy(
-        q_hbm.at[0, :, pl.ds(pl.multiple_of(split * width, width), width)], q_in, q_sem
+        q_hbm.at[0, :, pl.ds(pl.multiple_of(split * width, width), width)], q_in, in_sem.at[2]
     )
+    prefix_copy.start()
+    suffix_copy.start()
     q_copy.start()
+    prefix_copy.wait()
 
     kv[core, a3, y, a1, 0] = prefix_ref[:, :D]
     kv[core, a3, y, a1, 1] = prefix_ref[:, D:].astype(jnp.float32).T.astype(jnp.bfloat16)
+
+    pl.semaphore_wait(barrier, len(copies_here))
+
+    def remote(src, dst, send, recv, target):
+        return pltpu.make_async_remote_copy(
+            src_ref=src, dst_ref=dst, send_sem=send, recv_sem=recv, device_id=target, device_id_type=MESH
+        )
+
+    def first(d, other_core):
+        here = kv.at[core, a3, y, a1]
+        index = d + 4 * other_core
+        return remote(
+            here, here, send_sem.at[index], first_sem.at[(4 - d) % 4 + 4 * other_core],
+            device(d1=d, other_core=other_core),
+        )
+
+    def line_at(d3, d2):
+        return kv.at[core, (a3 + d3) % 4, (y + d2) % 4]
+
+    def line_copy(index, d3, d2, s3, s2):
+        ref = line_at(d3, d2)
+        landing = ((d3 - s3) % 4) * 4 + (d2 - s2) % 4
+        return remote(ref, ref, send_sem.at[8 + index], line_sem.at[landing], device(d3=s3 % 4, d2=s2 % 4))
+
+    def sib_copy(d3, d2):
+        ref = line_at(d3, d2)
+        return remote(ref, ref, send_sem.at[24 + d3 * 4 + d2], sib_sem.at[d3 * 4 + d2], sibling)
+
+    def other_copy():
+        return remote(suffix_ref, other, send_sem.at[0], first_sem.at[0], partner)
+
+    plan = [(0, 0, 1, 0), (0, 0, -1, 0), (0, 0, 0, 1), (0, 0, 0, -1), (0, 0, 2, 0), (0, 0, 0, 2)]
+    plan += [(0, d2, s3, 0) for d2 in (1, 3, 2) for s3 in (1, -1, 2)]
+
+    def event(d3, d2):
+        if (d3, d2) == (0, 0):
+            for d in (1, 2, 3):
+                first(d, 0).wait_recv()
+        else:
+            ref = line_at(d3, d2)
+            remote(ref, ref, send_sem.at[0], line_sem.at[d3 * 4 + d2], sibling).wait_recv()
+        for index, (e3, e2, s3, s2) in enumerate(plan):
+            if (e3, e2) == (d3, d2):
+                line_copy(index, e3, e2, s3, s2).start()
+        if (d3, d2) != (0, 0):
+            sib_copy(d3, d2).start()
+
+    def sib_wait(d3, d2):
+        if (d3, d2) == (0, 0):
+            for d in range(4):
+                first(d, 1).wait_recv()
+            return
+        ref = kv.at[1 - core, (a1 + d3) % 4, (y + d2) % 4]
+        remote(ref, ref, send_sem.at[0], sib_sem.at[d3 * 4 + d2], sibling).wait_recv()
+
+    for other_core in (0, 1):
+        for d in (1, 3, 2):
+            first(d, other_core).start()
+    first(0, 1).start()
+    suffix_copy.wait()
+    other_copy().start()
 
     m_ref[...] = jnp.full_like(m_ref, NEG)
     l_ref[...] = jnp.zeros_like(l_ref)
     acc[...] = jnp.zeros_like(acc)
     p1[...] = jnp.zeros_like(p1)
     c1[...] = jnp.ones_like(c1)
-
-    pl.semaphore_wait(barrier, 9)
-
-    def remote(src, dst, send, recv, target):
-        return pltpu.make_async_remote_copy(
-            src_ref=src, dst_ref=dst, send_sem=send, recv_sem=recv, device_id=target, device_id_type=MESH
-        )
-
-    def first(d):
-        here = kv.at[core, a3, y, a1]
-        return remote(here, here, send_sem.at[d - 1], recv_sem.at[3 - d], device(d1=d))
-
-    def line_at(d3, d2):
-        return kv.at[core, (a3 + d3) % 4, (y + d2) % 4]
-
-    sends = []
-
-    def line_copy(index, d3, d2, s3, s2):
-        ref = line_at(d3, d2)
-        landing = ((d3 - s3) % 4) * 4 + (d2 - s2) % 4
-        return remote(ref, ref, send_sem.at[3 + index], line_sem.at[landing], device(d3=s3 % 4, d2=s2 % 4))
-
-    def sib_copy(d3, d2):
-        ref = line_at(d3, d2)
-        return remote(ref, ref, send_sem.at[19 + d3 * 4 + d2], sib_sem.at[d3 * 4 + d2], sibling)
-
-    def other_copy():
-        return remote(suffix_ref.at[0], other, send_sem.at[18], recv_sem.at[3], partner)
-
-    plan = [
-        (0, 0, 0, 1), (0, 0, 0, -1), (0, 3, 0, 1),
-        (0, 0, 1, 0), (0, 0, -1, 0), (0, 1, 1, 0), (0, 1, -1, 0),
-        (0, 3, 1, 0), (0, 3, -1, 0), (0, 2, 1, 0), (0, 2, -1, 0),
-        (3, 0, 1, 0), (3, 1, 1, 0), (1, 2, -1, 0), (1, 3, -1, 0),
-    ]
-
-    def event(d3, d2):
-        if (d3, d2) == (0, 0):
-            for d in (1, 2, 3):
-                first(d).wait_recv()
-        else:
-            ref = line_at(d3, d2)
-            remote(ref, ref, send_sem.at[3], line_sem.at[d3 * 4 + d2], sibling).wait_recv()
-        for index, (e3, e2, s3, s2) in enumerate(plan):
-            if (e3, e2) == (d3, d2):
-                line_copy(index, e3, e2, s3, s2).start()
-        sib_copy(d3, d2).start()
-
-    def sib_wait(d3, d2):
-        ref = kv.at[1 - core, (a1 + d3) % 4, (y + d2) % 4]
-        remote(ref, ref, send_sem.at[3], sib_sem.at[d3 * 4 + d2], sibling).wait_recv()
-
-    for d in (1, 2, 3):
-        first(d).start()
-    other_copy().start()
-
     q_copy.wait()
     for h in range(heads):
         q_t[:, h * seq : (h + 1) * seq] = q_in[:, h * D : (h + 1) * D].astype(jnp.float32).T.astype(jnp.bfloat16)
@@ -157,11 +163,27 @@
     def values_of(ref):
         return ref[:, D:].astype(jnp.float32).T.astype(jnp.bfloat16)
 
-    own_part(suffix_ref[0, :, :D], values_of(suffix_ref.at[0]), split * tokens_here)
+    own_part(suffix_ref[:, :D], values_of(suffix_ref), split * tokens_here)
+
+    order = [
+        ((0, 0, 0), (1, 0, 0)), ((0, 1, 0), (0, 3, 0)), ((1, 1, 0), (1, 3, 0)), ((0, 2, 0), (0, 0, 1)),
+        ((0, 0, 3), (1, 2, 0)), ((1, 0, 1), (1, 0, 3)), ((0, 0, 2), (1, 0, 2)), ((0, 1, 1), (0, 3, 1)),
+        ((1, 1, 1), (1, 3, 1)), ((0, 1, 3), (0, 3, 3)), ((1, 1, 3), (1, 3, 3)), ((0, 2, 1), (1, 2, 1)),
+        ((0, 2, 3), (1, 2, 3)), ((0, 1, 2), (1, 1, 2)), ((0, 3, 2), (1, 3, 2)), ((0, 2, 2), (1, 2, 2)),
+    ]
+
+    def packed(k, part, i):
+        word = sum(step[k][part] << (2 * at) for at, step in enumerate(order))
+        word = word - (1 << 32) if word >= 1 << 31 else word
+        return (jnp.int32(word) >> (2 * i)) & 3
 
     def lines(i):
-        d3, d2 = gray(i // 4), gray(i % 4)
-        return (core, (a3 + d3) % 4, (y + d2) % 4), (1 - core, (a1 + d3) % 4, (y + d2) % 4)
+        found = []
+        for k in (0, 1):
+            stream, d3, d2 = (packed(k, part, i) for part in range(3))
+            base = a3 * (1 - stream) + a1 * stream
+            found.append((core + stream * (1 - 2 * core), (base + d3) % 4, (y + d2) % 4))
+        return found
 
     def keys_of(i, j):
         c, l3, l2 = lines(i)[j // 2]
@@ -206,15 +228,19 @@
         acc[:, cols(pb)] = acc[:, cols(pb)] * fixes[nbuf][...] + add
 
     handed = {
-        0: [(0, 3), (0, 1), (3, 0), (1, 0)],
-        1: [(3, 1), (1, 3), (3, 3), (1, 1)],
-        2: [(0, 2), (2, 0)],
-        3: [(3, 2), (1, 2)],
-        4: [(2, 1), (2, 3)],
-        5: [(2, 2)],
+        (0, 7): [(1, 0), (3, 0)],
+        (1, 7): [(0, 1), (0, 3), (2, 0)],
+        (3, 4): [(0, 2)],
+        (4, 0): [(1, 1), (3, 1)],
+        (5, 0): [(1, 3), (3, 3)],
+        (6, 0): [(2, 1), (2, 3)],
+        (7, 0): [(1, 2), (3, 2)],
+        (8, 0): [(2, 2)],
     }
 
     event(0, 0)
+    other_copy().wait_recv()
+    own_part(other[:, :D], values_of(other), (1 - split) * tokens_here)
     sib_wait(0, 0)
     top = None
     for j in range(PIECES):
@@ -223,26 +249,25 @@
 
     def body(i, carry):
         for b in range(units):
-            if b == units // 2:
-                for step, group in handed.items():
+            for (step, place), group in handed.items():
+                if place == b:
                     @pl.when(i == step)
                     def _(group=group):
                         for d3, d2 in group:
                             event(d3, d2)
             if b == units - 1:
-                for step in range(1, 16):
+                for step in [k for k in range(1, 16) if order[k][0][0] + order[k][1][0]]:
                     @pl.when(i + 1 == step)
                     def _(step=step):
-                        sib_wait(gray(step // 4), gray(step % 4))
+                        for stream, d3, d2 in order[step]:
+                            if stream == 1:
+                                sib_wait(d3, d2)
             unit(i, b)
         return carry
 
     lax.fori_loop(0, 16, body, 0)
     pb = units - 1
     acc[:, cols(pb)] = acc[:, cols(pb)] * fixes[pb % 2][...] + pv(last, pb % 2)
-
-    other_copy().wait_recv()
-    own_part(other[:, :D], values_of(other), (1 - split) * tokens_here)
 
     for h in range(heads):
         part = slice(h * seq, (h + 1) * seq)
@@ -250,13 +275,16 @@
         out_ref[0, :, h * D : (h + 1) * D] = (acc[:, part] * inverse).T.astype(jnp.bfloat16)
 
     for d in (1, 2, 3):
-        first(d).wait_send()
+        first(d, 0).wait_send()
+    for d in range(4):
+        first(d, 1).wait_send()
     other_copy().wait_send()
     for index, (e3, e2, s3, s2) in enumerate(plan):
         line_copy(index, e3, e2, s3, s2).wait_send()
     for d3 in range(4):
         for d2 in range(4):
-            sib_copy(d3, d2).wait_send()
+            if (d3, d2) != (0, 0):
+                sib_copy(d3, d2).wait_send()
 
 
 def shards(queries, prefix_kv, suffix_kv):
@@ -267,12 +295,14 @@
     return pl.pallas_call(
         kernel,
         out_shape=jax.ShapeDtypeStruct((suf_count, seq, half), jnp.bfloat16),
-        in_specs=[pl.BlockSpec(memory_space=pl.ANY), vmem, vmem],
+        in_specs=[pl.BlockSpec(memory_space=pltpu.HBM)] * 3,
         out_specs=vmem,
         scratch_shapes=[
             pltpu.VMEM((2, 4, 4, LINE, 2, BLOCK, D), jnp.bfloat16),
             pltpu.VMEM((seq, half), jnp.bfloat16),
             pltpu.VMEM((D, rows), jnp.bfloat16),
+            pltpu.VMEM(prefix_kv.shape, jnp.bfloat16),
+            pltpu.VMEM(suffix_kv.shape[1:], jnp.bfloat16),
             pltpu.VMEM(suffix_kv.shape[1:], jnp.bfloat16),
             pltpu.VMEM((TOKENS, LANES), jnp.float32),
             pltpu.VMEM((TOKENS, LANES), jnp.float32),
@@ -285,14 +315,14 @@
             pltpu.VMEM((1, rows), jnp.float32),
             pltpu.VMEM((SUB, rows), jnp.float32),
             pltpu.VMEM((D, rows), jnp.float32),
-            pltpu.SemaphoreType.DMA,
-            pltpu.SemaphoreType.DMA((35,)),
-            pltpu.SemaphoreType.DMA((4,)),
+            pltpu.SemaphoreType.DMA((3,)),
+            pltpu.SemaphoreType.DMA((40,)),
+            pltpu.SemaphoreType.DMA((8,)),
             pltpu.SemaphoreType.DMA((16,)),
             pltpu.SemaphoreType.DMA((16,)),
         ],
         compiler_params=pltpu.CompilerParams(
-            collective_id=0, has_side_effects=True, vmem_limit_bytes=48 * 2**20
+            collective_id=0, has_side_effects=True, vmem_limit_bytes=60 * 2**20
         ),
         cost_estimate=pl.CostEstimate(flops=17 * 10**9, bytes_accessed=2 * 2**20, transcendentals=34 * 10**6),
     )(queries, prefix_kv, suffix_kv)

time: 84.9 us -> 75.3 us (0.89); the launches traced: 84.7 us -> 74.2 us
  Pallas kernels: 80.9 us -> 72.3 us
  local copies, waits for them, and re-layouts: 3.76 us -> 1.87 us
    pallas_call x1, Pallas kernels: 80.9 us -> 72.3 us  [shards(): pl.pallas_call(kernel, out_shape=jax.ShapeDtypeStruct((suf_count, seq, ha...]
    unnamed x7 -> x1, local copies, waits for them, and re-layouts: 3.76 us -> 1.87 us
where the time goes in v2:
time: 75.3 us; the launch traced here: 74.2 us
  Pallas kernels  72.3 us (96%)
  local copies, waits for them, and re-layouts  1.87 us (2%)
    pallas_call x1, Pallas kernels, shards(): pl.pallas_call(kernel, out_shape=jax.ShapeDtypeStruct((suf_count, seq, ha...  72.3 us
    unnamed x1, local copies, waits for them, and re-layouts  1.87 us

profile of v2, /device:TPU:1, one launch (start us, length us, event | category | flops | bytes accessed | tf_op | source)
XLA Modules:
  0.0 74.2 jit_solution(17618065898038383509)
XLA Ops:
  0.0 72.3 %shard_map.37 = bf16[1,512,512]{2,1,0:T(8,128)(2,1)} custom-call(bf16[1,512,1024]{2,1,0:T(8,128)(2,1)} %q_hbm.1, bf16[128,256]{1,0:T(8,128)(2,1)} %prefix_hbm.1, bf16[1,256,256]{2,1,0:T(8,128)(2,1)} %suffix_hbm.1), custom_call_target="tpu_custom_call" | custom-call | flops 16999999488 | bytes 2097152 | tf_op jit(solution)/shard_map/pallas_call | solution.py:295
  72.3 1.9 %copy.5 = bf16[1,512,512]{2,1,0:T(8,128)(2,1)} copy(bf16[1,512,512]{2,1,0:T(8,128)(2,1)} %shard_map.37) | data formatting | bytes 1048576

commit v3 on v2

--- a/solution.py
+++ b/solution.py
@@ -132,8 +132,10 @@
     m_ref[...] = jnp.full_like(m_ref, NEG)
     l_ref[...] = jnp.zeros_like(l_ref)
     acc[...] = jnp.zeros_like(acc)
-    p1[...] = jnp.zeros_like(p1)
-    c1[...] = jnp.ones_like(c1)
+    s1[...] = jnp.full_like(s1, NEG)
+    x1[...] = jnp.full_like(x1, NEG)
+    p0[...] = jnp.zeros_like(p0)
+    c0[...] = jnp.ones_like(c0)
     q_copy.wait()
     for h in range(heads):
         q_t[:, h * seq : (h + 1) * seq] = q_in[:, h * D : (h + 1) * D].astype(jnp.float32).T.astype(jnp.bfloat16)
@@ -202,72 +204,65 @@
             parts += [kv[c, l3, l2, k, 1] for k in range(LINE)]
         return jnp.dot(jnp.concatenate(parts, axis=1), weights[buf][...], preferred_element_type=jnp.float32)
 
-    last = 15
-
-    def unit(i, b):
-        ni, nb = (i, b + 1) if b < units - 1 else (jnp.minimum(i + 1, last), 0)
-        pi, pb = (i, b - 1) if b > 0 else (jnp.maximum(i - 1, 0), units - 1)
-        buf, nbuf = b % 2, (b + 1) % 2
+    def softmax_begin(b):
+        buf = b % 2
         m_old = m_ref[:, cols(b)]
         m_new = jnp.maximum(m_old, jnp.max(tops[buf][...], axis=0, keepdims=True) * scale)
         fix = jnp.exp2(m_old - m_new)
         m_ref[:, cols(b)] = m_new
         fixes[buf][...] = fix
-        total = l_ref[:, cols(b)] * fix
-        top, add = None, None
+        return m_new, l_ref[:, cols(b)] * fix
+
+    def softmax_piece(b, j, m_new, total):
+        buf = b % 2
+        part = slice(j * PIECE, (j + 1) * PIECE)
+        p = jnp.exp2(scores[buf][part, :] * scale - m_new)
+        weights[buf][part, :] = p.astype(jnp.bfloat16)
+        return total + jnp.sum(p.reshape(-1, SUB, LANES), axis=0)
+
+    def unit(i, b):
+        b1, b2 = (b - 1) % units, (b - 2) % units
+        before = jnp.maximum(i - 1, 0)
+        m_new, total = softmax_begin(b1)
+        top, add, fix = None, None, None
         for j in range(PIECES):
-            top = qk(ni, nb, nbuf, j, top)
+            top = qk(i, b, b % 2, j, top)
             if j == 0:
-                add = pv(pi, nbuf)
-            part = slice(j * PIECE, (j + 1) * PIECE)
-            p = jnp.exp2(scores[buf][part, :] * scale - m_new)
-            weights[buf][part, :] = p.astype(jnp.bfloat16)
-            total = total + jnp.sum(p.reshape(-1, SUB, LANES), axis=0)
-        tops[nbuf][...] = top
-        l_ref[:, cols(b)] = total
-        acc[:, cols(pb)] = acc[:, cols(pb)] * fixes[nbuf][...] + add
-
-    handed = {
-        (0, 7): [(1, 0), (3, 0)],
-        (1, 7): [(0, 1), (0, 3), (2, 0)],
-        (3, 4): [(0, 2)],
-        (4, 0): [(1, 1), (3, 1)],
-        (5, 0): [(1, 3), (3, 3)],
-        (6, 0): [(2, 1), (2, 3)],
-        (7, 0): [(1, 2), (3, 2)],
-        (8, 0): [(2, 2)],
-    }
+                fix = fixes[b % 2][...]
+                add = pv(i if b >= 2 else before, b % 2)
+            total = softmax_piece(b1, j, m_new, total)
+        tops[b % 2][...] = top
+        l_ref[:, cols(b1)] = total
+        acc[:, cols(b2)] = acc[:, cols(b2)] * fix + add
+
+    handed = {1: [(1, 0), (3, 0)], 3: [(0, 1), (0, 3), (2, 0)], 5: [(0, 2)], 7: [(1, 1), (3, 1), (1, 3), (3, 3)], 9: [(2, 1), (2, 3)], 11: [(1, 2), (3, 2), (2, 2)]}
 
     event(0, 0)
     other_copy().wait_recv()
     own_part(other[:, :D], values_of(other), (1 - split) * tokens_here)
-    sib_wait(0, 0)
-    top = None
-    for j in range(PIECES):
-        top = qk(0, 0, 0, j, top)
-    tops[0][...] = top
 
     def body(i, carry):
+        for step in range(16):
+            waits = [line[1:] for line in order[step] if line[0] == 1]
+            if waits or step in handed:
+                @pl.when(i == step)
+                def _(step=step, waits=waits):
+                    for d3, d2 in handed.get(step, []):
+                        event(d3, d2)
+                    for d3, d2 in waits:
+                        sib_wait(d3, d2)
         for b in range(units):
-            for (step, place), group in handed.items():
-                if place == b:
-                    @pl.when(i == step)
-                    def _(group=group):
-                        for d3, d2 in group:
-                            event(d3, d2)
-            if b == units - 1:
-                for step in [k for k in range(1, 16) if order[k][0][0] + order[k][1][0]]:
-                    @pl.when(i + 1 == step)
-                    def _(step=step):
-                        for stream, d3, d2 in order[step]:
-                            if stream == 1:
-                                sib_wait(d3, d2)
             unit(i, b)
         return carry
 
     lax.fori_loop(0, 16, body, 0)
-    pb = units - 1
-    acc[:, cols(pb)] = acc[:, cols(pb)] * fixes[pb % 2][...] + pv(last, pb % 2)
+    for b in (units - 2, units - 1):
+        if b == units - 1:
+            m_new, total = softmax_begin(b)
+            for j in range(PIECES):
+                total = softmax_piece(b, j, m_new, total)
+            l_ref[:, cols(b)] = total
+        acc[:, cols(b)] = acc[:, cols(b)] * fixes[b % 2][...] + pv(15, b % 2)
 
     for h in range(heads):
         part = slice(h * seq, (h + 1) * seq)

time: 75.3 us -> 68.7 us (0.912)
  Pallas kernels: 72.3 us -> 65.9 us
    pallas_call x1, Pallas kernels: 72.3 us -> 65.9 us  [shards(): pl.pallas_call(kernel, out_shape=jax.ShapeDtypeStruct((suf_count, seq, ha...]
where the time goes in v3:
time: 68.7 us; the launch traced here: 67.8 us
  Pallas kernels  65.9 us (96%)
  local copies, waits for them, and re-layouts  1.87 us (3%)
    pallas_call x1, Pallas kernels, shards(): pl.pallas_call(kernel, out_shape=jax.ShapeDtypeStruct((suf_count, seq, ha...  65.9 us
    unnamed x1, local copies, waits for them, and re-layouts  1.87 us

profile of v3, /device:TPU:1, one launch (start us, length us, event | category | flops | bytes accessed | tf_op | source)
XLA Modules:
  0.0 67.8 jit_solution(7871350057791703450)
XLA Ops:
  0.0 65.9 %shard_map.37 = bf16[1,512,512]{2,1,0:T(8,128)(2,1)} custom-call(bf16[1,512,1024]{2,1,0:T(8,128)(2,1)} %q_hbm.1, bf16[128,256]{1,0:T(8,128)(2,1)} %prefix_hbm.1, bf16[1,256,256]{2,1,0:T(8,128)(2,1)} %suffix_hbm.1), custom_call_target="tpu_custom_call" | custom-call | flops 16999999488 | bytes 2097152 | tf_op jit(solution)/shard_map/pallas_call | solution.py:290
  66.0 1.9 %copy.5 = bf16[1,512,512]{2,1,0:T(8,128)(2,1)} copy(bf16[1,512,512]{2,1,0:T(8,128)(2,1)} %shard_map.37) | data formatting | bytes 1048576

commit v4 on v3

--- a/solution.py
+++ b/solution.py
@@ -23,11 +23,11 @@
 
 def kernel(
     q_hbm, prefix_hbm, suffix_hbm, out_ref,
-    kv, q_in, q_t, prefix_ref, suffix_ref, other, s0, s1, p0, p1, x0, x1, c0, c1, m_ref, l_ref, acc,
+    kv, q_in, q_t, prefix_ref, suffix_ref, other, s0, s1, x0, x1, m_ref, l_ref, acc,
     in_sem, send_sem, first_sem, line_sem, sib_sem,
 ):
     scale = LOG2E / math.sqrt(D)
-    scores, weights, tops, fixes = (s0, s1), (p0, p1), (x0, x1), (c0, c1)
+    scores, tops = (s0, s1), (x0, x1)
     tokens_here = suffix_ref.shape[0]
     seq, width = q_in.shape
     heads = width // D
@@ -65,8 +65,9 @@
     q_copy.start()
     prefix_copy.wait()
 
-    kv[core, a3, y, a1, 0] = prefix_ref[:, :D]
-    kv[core, a3, y, a1, 1] = prefix_ref[:, D:].astype(jnp.float32).T.astype(jnp.bfloat16)
+    own_line = core * 16 + a3 * 4 + y
+    kv[own_line, a1, 0] = prefix_ref[:, :D]
+    kv[own_line, a1, 1] = prefix_ref[:, D:].astype(jnp.float32).T.astype(jnp.bfloat16)
 
     pl.semaphore_wait(barrier, len(copies_here))
 
@@ -76,7 +77,7 @@
         )
 
     def first(d, other_core):
-        here = kv.at[core, a3, y, a1]
+        here = kv.at[own_line, a1]
         index = d + 4 * other_core
         return remote(
             here, here, send_sem.at[index], first_sem.at[(4 - d) % 4 + 4 * other_core],
@@ -84,7 +85,7 @@
         )
 
     def line_at(d3, d2):
-        return kv.at[core, (a3 + d3) % 4, (y + d2) % 4]
+        return kv.at[core * 16 + (a3 + d3) % 4 * 4 + (y + d2) % 4]
 
     def line_copy(index, d3, d2, s3, s2):
         ref = line_at(d3, d2)
@@ -119,7 +120,7 @@
             for d in range(4):
                 first(d, 1).wait_recv()
             return
-        ref = kv.at[1 - core, (a1 + d3) % 4, (y + d2) % 4]
+        ref = kv.at[(1 - core) * 16 + (a1 + d3) % 4 * 4 + (y + d2) % 4]
         remote(ref, ref, send_sem.at[0], sib_sem.at[d3 * 4 + d2], sibling).wait_recv()
 
     for other_core in (0, 1):
@@ -134,8 +135,6 @@
     acc[...] = jnp.zeros_like(acc)
     s1[...] = jnp.full_like(s1, NEG)
     x1[...] = jnp.full_like(x1, NEG)
-    p0[...] = jnp.zeros_like(p0)
-    c0[...] = jnp.ones_like(c0)
     q_copy.wait()
     for h in range(heads):
         q_t[:, h * seq : (h + 1) * seq] = q_in[:, h * D : (h + 1) * D].astype(jnp.float32).T.astype(jnp.bfloat16)
@@ -184,62 +183,55 @@
         for k in (0, 1):
             stream, d3, d2 = (packed(k, part, i) for part in range(3))
             base = a3 * (1 - stream) + a1 * stream
-            found.append((core + stream * (1 - 2 * core), (base + d3) % 4, (y + d2) % 4))
+            found.append((core + stream * (1 - 2 * core)) * 16 + ((base + d3) & 3) * 4 + ((y + d2) & 3))
         return found
 
-    def keys_of(i, j):
-        c, l3, l2 = lines(i)[j // 2]
+    def keys_of(pair, j):
         k = 2 * (j % 2)
-        return kv[c, l3, l2, pl.ds(k, 2), 0].reshape(PIECE, D)
-
-    def qk(i, b, buf, j, top):
-        s = jnp.dot(keys_of(i, j), q_t[:, cols(b)], preferred_element_type=jnp.float32)
+        return kv[pair[j // 2], k : k + 2, 0].reshape(PIECE, D)
+
+    def qk(pair, b, buf, j, top):
+        s = jnp.dot(keys_of(pair, j), q_t[:, cols(b)], preferred_element_type=jnp.float32)
         scores[buf][j * PIECE : (j + 1) * PIECE, :] = s
         here = tile_max(s)
         return here if top is None else jnp.maximum(top, here)
 
-    def pv(i, buf):
-        parts = []
-        for c, l3, l2 in lines(i):
-            parts += [kv[c, l3, l2, k, 1] for k in range(LINE)]
-        return jnp.dot(jnp.concatenate(parts, axis=1), weights[buf][...], preferred_element_type=jnp.float32)
+    def values_piece(pair, j):
+        k = 2 * (j % 2)
+        return jnp.concatenate([kv[pair[j // 2], k, 1], kv[pair[j // 2], k + 1, 1]], axis=1)
+
+    def unit(pair, before, b):
+        b1 = (b - 1) % units
+        buf, buf1 = b % 2, (b - 1) % 2
+        values_pair = before if b == 0 else pair
+        m_new, fix, total = softmax_begin(b1)
+        top, add = None, None
+        for j in range(PIECES):
+            p, total = softmax_piece(b1, j, m_new, total)
+            top = qk(pair, b, buf, j, top)
+            here = jnp.dot(values_piece(values_pair, j), p, preferred_element_type=jnp.float32)
+            add = here if add is None else add + here
+        tops[buf][...] = top
+        softmax_end(b1, fix, total, add)
 
     def softmax_begin(b):
-        buf = b % 2
         m_old = m_ref[:, cols(b)]
-        m_new = jnp.maximum(m_old, jnp.max(tops[buf][...], axis=0, keepdims=True) * scale)
+        m_new = jnp.maximum(m_old, jnp.max(tops[b % 2][...], axis=0, keepdims=True) * scale)
         fix = jnp.exp2(m_old - m_new)
         m_ref[:, cols(b)] = m_new
-        fixes[buf][...] = fix
-        return m_new, l_ref[:, cols(b)] * fix
+        return m_new, fix, l_ref[:, cols(b)] * fix
 
     def softmax_piece(b, j, m_new, total):
-        buf = b % 2
-        part = slice(j * PIECE, (j + 1) * PIECE)
-        p = jnp.exp2(scores[buf][part, :] * scale - m_new)
-        weights[buf][part, :] = p.astype(jnp.bfloat16)
-        return total + jnp.sum(p.reshape(-1, SUB, LANES), axis=0)
-
-    def unit(i, b):
-        b1, b2 = (b - 1) % units, (b - 2) % units
-        before = jnp.maximum(i - 1, 0)
-        m_new, total = softmax_begin(b1)
-        top, add, fix = None, None, None
-        for j in range(PIECES):
-            top = qk(i, b, b % 2, j, top)
-            if j == 0:
-                fix = fixes[b % 2][...]
-                add = pv(i if b >= 2 else before, b % 2)
-            total = softmax_piece(b1, j, m_new, total)
-        tops[b % 2][...] = top
-        l_ref[:, cols(b1)] = total
-        acc[:, cols(b2)] = acc[:, cols(b2)] * fix + add
+        p = jnp.exp2(scores[b % 2][j * PIECE : (j + 1) * PIECE, :] * scale - m_new)
+        return p.astype(jnp.bfloat16), total + jnp.sum(p.reshape(-1, SUB, LANES), axis=0)
+
+    def softmax_end(b, fix, total, add):
+        l_ref[:, cols(b)] = total
+        acc[:, cols(b)] = acc[:, cols(b)] * fix + add
 
     handed = {1: [(1, 0), (3, 0)], 3: [(0, 1), (0, 3), (2, 0)], 5: [(0, 2)], 7: [(1, 1), (3, 1), (1, 3), (3, 3)], 9: [(2, 1), (2, 3)], 11: [(1, 2), (3, 2), (2, 2)]}
 
     event(0, 0)
-    other_copy().wait_recv()
-    own_part(other[:, :D], values_of(other), (1 - split) * tokens_here)
 
     def body(i, carry):
         for step in range(16):
@@ -247,22 +239,27 @@
             if waits or step in handed:
                 @pl.when(i == step)
                 def _(step=step, waits=waits):
+                    if step == 1:
+                        other_copy().wait_recv()
+                        own_part(other[:, :D], values_of(other), (1 - split) * tokens_here)
                     for d3, d2 in handed.get(step, []):
                         event(d3, d2)
                     for d3, d2 in waits:
                         sib_wait(d3, d2)
+        pair, before = lines(i), lines(jnp.maximum(i - 1, 0))
         for b in range(units):
-            unit(i, b)
+            unit(pair, before, b)
         return carry
 
     lax.fori_loop(0, 16, body, 0)
-    for b in (units - 2, units - 1):
-        if b == units - 1:
-            m_new, total = softmax_begin(b)
-            for j in range(PIECES):
-                total = softmax_piece(b, j, m_new, total)
-            l_ref[:, cols(b)] = total
-        acc[:, cols(b)] = acc[:, cols(b)] * fixes[b % 2][...] + pv(15, b % 2)
+    b = units - 1
+    m_new, fix, total = softmax_begin(b)
+    add = None
+    for j in range(PIECES):
+        p, total = softmax_piece(b, j, m_new, total)
+        here = jnp.dot(values_piece(lines(15), j), p, preferred_element_type=jnp.float32)
+        add = here if add is None else add + here
+    softmax_end(b, fix, total, add)
 
     for h in range(heads):
         part = slice(h * seq, (h + 1) * seq)
@@ -293,7 +290,7 @@
         in_specs=[pl.BlockSpec(memory_space=pltpu.HBM)] * 3,
         out_specs=vmem,
         scratch_shapes=[
-            pltpu.VMEM((2, 4, 4, LINE, 2, BLOCK, D), jnp.bfloat16),
+            pltpu.VMEM((32, LINE, 2, BLOCK, D), jnp.bfloat16),
             pltpu.VMEM((seq, half), jnp.bfloat16),
             pltpu.VMEM((D, rows), jnp.bfloat16),
             pltpu.VMEM(prefix_kv.shape, jnp.bfloat16),
@@ -301,12 +298,8 @@
             pltpu.VMEM(suffix_kv.shape[1:], jnp.bfloat16),
             pltpu.VMEM((TOKENS, LANES), jnp.float32),
             pltpu.VMEM((TOKENS, LANES), jnp.float32),
-            pltpu.VMEM((TOKENS, LANES), jnp.bfloat16),
-            pltpu.VMEM((TOKENS, LANES), jnp.bfloat16),
             pltpu.VMEM((SUB, LANES), jnp.float32),
             pltpu.VMEM((SUB, LANES), jnp.float32),
-            pltpu.VMEM((1, LANES), jnp.float32),
-            pltpu.VMEM((1, LANES), jnp.float32),
             pltpu.VMEM((1, rows), jnp.float32),
             pltpu.VMEM((SUB, rows), jnp.float32),
             pltpu.VMEM((D, rows), jnp.float32),

time: 68.7 us -> 66.9 us (0.974); the launches traced: 67.8 us -> 66.7 us
  Pallas kernels: 65.9 us -> 64.9 us
    pallas_call x1, Pallas kernels: 65.9 us -> 64.9 us  [shards(): pl.pallas_call(kernel, out_shape=jax.ShapeDtypeStruct((suf_count, seq, ha...]
where the time goes in v4:
time: 66.9 us; the launch traced here: 66.7 us
  Pallas kernels  64.9 us (97%)
  local copies, waits for them, and re-layouts  1.87 us (3%)
    pallas_call x1, Pallas kernels, shards(): pl.pallas_call(kernel, out_shape=jax.ShapeDtypeStruct((suf_count, seq, ha...  64.9 us
    unnamed x1, local copies, waits for them, and re-layouts  1.87 us

profile of v4, /device:TPU:1, one launch (start us, length us, event | category | flops | bytes accessed | tf_op | source)
XLA Modules:
  0.0 66.7 jit_solution(11265170227827332693)
XLA Ops:
  0.0 64.9 %shard_map.37 = bf16[1,512,512]{2,1,0:T(8,128)(2,1)} custom-call(bf16[1,512,1024]{2,1,0:T(8,128)(2,1)} %q_hbm.1, bf16[128,256]{1,0:T(8,128)(2,1)} %prefix_hbm.1, bf16[1,256,256]{2,1,0:T(8,128)(2,1)} %suffix_hbm.1), custom_call_target="tpu_custom_call" | custom-call | flops 16999999488 | bytes 2097152 | tf_op jit(solution)/shard_map/pallas_call | solution.py:287
  64.9 1.9 %copy.5 = bf16[1,512,512]{2,1,0:T(8,128)(2,1)} copy(bf16[1,512,512]{2,1,0:T(8,128)(2,1)} %shard_map.37) | data formatting | bytes 1048576

commit v5 on v4

--- a/solution.py
+++ b/solution.py
@@ -49,12 +49,6 @@
     a3 = z * (1 - core) + x * core
     sibling = device(other_core=1)
     partner = ((x * 16 + (z % 2) * 8 + y * 2 + core), 1 - split)
-    copies_here = [device(**{axis: d}) for axis in ("d1", "d2", "d3") for d in (1, 2, 3)]
-    copies_here += [device(d3=d, other_core=1) for d in (1, 2, 3)] + [sibling, partner]
-    barrier = pltpu.get_barrier_semaphore()
-    for peer in copies_here:
-        pl.semaphore_signal(barrier, inc=1, device_id=peer, device_id_type=MESH)
-
     prefix_copy = pltpu.make_async_copy(prefix_hbm, prefix_ref, in_sem.at[0])
     suffix_copy = pltpu.make_async_copy(suffix_hbm.at[0], suffix_ref, in_sem.at[1])
     q_copy = pltpu.make_async_copy(
@@ -63,6 +57,12 @@
     prefix_copy.start()
     suffix_copy.start()
     q_copy.start()
+    copies_here = [device(**{axis: d}) for axis in ("d1", "d2", "d3") for d in (1, 2, 3)]
+    copies_here += [device(d3=d, other_core=1) for d in (1, 2, 3)] + [sibling, partner]
+    barrier = pltpu.get_barrier_semaphore()
+    for peer in copies_here:
+        pl.semaphore_signal(barrier, inc=1, device_id=peer, device_id_type=MESH)
+
     prefix_copy.wait()
 
     own_line = core * 16 + a3 * 4 + y
@@ -146,7 +146,15 @@
         return jnp.max(s.reshape(s.shape[0] // SUB, SUB, LANES), axis=0)
 
     def own_part(keys, values_t, offset):
-        for b in range(units):
+        late = [b for b in range(units) if (b * LANES) % seq + LANES > tokens_here]
+        own_blocks(late, keys, values_t, offset)
+
+        @pl.when(offset == 0)
+        def _():
+            own_blocks([b for b in range(units) if b not in late], keys, values_t, offset)
+
+    def own_blocks(blocks, keys, values_t, offset):
+        for b in blocks:
             s = jnp.dot(keys, q_t[:, cols(b)], preferred_element_type=jnp.float32)
             u = lax.broadcasted_iota(jnp.int32, s.shape, 0) + offset
             t = lax.broadcasted_iota(jnp.int32, s.shape, 1) + (b * LANES) % seq
@@ -229,7 +237,7 @@
         l_ref[:, cols(b)] = total
         acc[:, cols(b)] = acc[:, cols(b)] * fix + add
 
-    handed = {1: [(1, 0), (3, 0)], 3: [(0, 1), (0, 3), (2, 0)], 5: [(0, 2)], 7: [(1, 1), (3, 1), (1, 3), (3, 3)], 9: [(2, 1), (2, 3)], 11: [(1, 2), (3, 2), (2, 2)]}
+    handed = {1: [(1, 0), (3, 0)], 3: [(0, 1), (0, 3), (2, 0)], 5: [(0, 2)], 6: [(1, 1), (3, 1)], 8: [(1, 3), (3, 3)], 9: [(2, 1), (2, 3)], 11: [(1, 2), (3, 2)], 13: [(2, 2)]}
 
     event(0, 0)
 

time: 66.9 us -> 67 us (level)
  no operation moved by 1% of the time
where the time goes in v5:
time: 67 us; the launch traced here: 66.8 us
  Pallas kernels  65 us (97%)
  local copies, waits for them, and re-layouts  1.87 us (3%)
    pallas_call x1, Pallas kernels, shards(): pl.pallas_call(kernel, out_shape=jax.ShapeDtypeStruct((suf_count, seq, ha...  65 us
    unnamed x1, local copies, waits for them, and re-layouts  1.87 us

profile of v5, /device:TPU:1, one launch (start us, length us, event | category | flops | bytes accessed | tf_op | source)
XLA Modules:
  0.0 66.8 jit_solution(11143179134237767392)
XLA Ops:
  0.0 65.0 %shard_map.37 = bf16[1,512,512]{2,1,0:T(8,128)(2,1)} custom-call(bf16[1,512,1024]{2,1,0:T(8,128)(2,1)} %q_hbm.1, bf16[128,256]{1,0:T(8,128)(2,1)} %prefix_hbm.1, bf16[1,256,256]{2,1,0:T(8,128)(2,1)} %suffix_hbm.1), custom_call_target="tpu_custom_call" | custom-call | flops 16999999488 | bytes 2097152 | tf_op jit(solution)/shard_map/pallas_call | solution.py:295
  65.0 1.9 %copy.5 = bf16[1,512,512]{2,1,0:T(8,128)(2,1)} copy(bf16[1,512,512]{2,1,0:T(8,128)(2,1)} %shard_map.37) | data formatting | bytes 1048576
